TPU v7x, 32 devices: a whole 2x2x4 slice. The times are simulated.
32 devices in a mesh: section: 2 (over x), batch: 16 (over z, y, core).
Axes of the slice: x: 2, y: 2, z: 4, core: 2. Of those that a mesh axis runs over, the one named last changes fastest.
Arguments:
- latents: bfloat16 [12288, 512], P('batch'), may hold values from 0 to 0.25
- actions: bfloat16 [2, 12288, 6], P('section', 'batch'), may hold values from -1 to 1
- tasks: int32 [12288], P('batch'), may hold values from 0 to 79
- masks: int32 [2, 12288], P('section', 'batch'), may hold values 0 or 1
- reward_bins: int32 [2, 12288], P('section', 'batch'), may hold values from 0 to 99
- reward_frac: float32 [2, 12288], P('section', 'batch'), may hold values from 0 to 1
- value_bins: int32 [2, 12288], P('section', 'batch'), may hold values from 0 to 99
- value_frac: float32 [2, 12288], P('section', 'batch'), may hold values from 0 to 1
- targets: bfloat16 [2, 12288, 512], P('section', 'batch'), may hold values from 0 to 0.25
- task_table: bfloat16 [80, 96], replicated, may hold values from -6 to 6
- w_latent: bfloat16 [2, 512, 7168], P('section'), may hold values from -2 to 2
- w_action: bfloat16 [2, 6, 7168], P('section'), may hold values from -4 to 4
- w_task: bfloat16 [2, 96, 7168], P('section'), may hold values from -0.625 to 0.625
- gain_one: float32 [2, 7168], P('section'), may hold values from 0.5 to 1.5
- shift_one: float32 [2, 7168], P('section'), may hold values from -1.8 to 1.8
- w_hidden: bfloat16 [2, 7, 1024, 1024], P('section'), may hold values from -0.1875 to 0.1875
- gain_two: float32 [2, 7, 1024], P('section'), may hold values from 0.5 to 1.5
- shift_two: float32 [2, 7, 1024], P('section'), may hold values from -1.8 to 1.8
- w_next: bfloat16 [2, 1024, 512], P('section'), may hold values from -0.1875 to 0.1875
- bias_next: float32 [2, 512], P('section'), may hold values from -3 to 3
- gain_three: float32 [2, 512], P('section'), may hold values from 0.5 to 1.5
- shift_three: float32 [2, 512], P('section'), may hold values from -1.8 to 1.8
- w_head: bfloat16 [2, 6, 1024, 101], P('section'), may hold values from -0.375 to 0.375
- bias_head: float32 [2, 6, 101], P('section'), may hold values from -3 to 3
Outputs:
- latents_out: bfloat16 [2, 12288, 512], P('section', 'batch')
- latent_grads: bfloat16 [2, 12288, 512], P('section', 'batch')
- step_loss: float32 [2], P('section')
- w_latent_grad: float32 [2, 512, 7168], P('section', None, 'batch')
- w_action_grad: float32 [2, 6, 7168], P('section', None, 'batch')
- w_task_grad: float32 [2, 96, 7168], P('section', None, 'batch')
- gain_one_grad: float32 [2, 7168], P('section', 'batch')
- shift_one_grad: float32 [2, 7168], P('section', 'batch')
- w_hidden_grad: float32 [2, 7, 1024, 1024], P('section', None, None, 'batch')
- gain_two_grad: float32 [2, 7, 1024], P('section', None, 'batch')
- shift_two_grad: float32 [2, 7, 1024], P('section', None, 'batch')
- w_next_grad: float32 [2, 1024, 512], P('section', 'batch')
- bias_next_grad: float32 [2, 512], P('section', 'batch')
- gain_three_grad: float32 [2, 512], P('section', 'batch')
- shift_three_grad: float32 [2, 512], P('section', 'batch')
- w_head_grad: float32 [2, 6, 1024, 101], P('section', None, 'batch')
- bias_head_grad: float32 [2, 6, 101], P('section')
- table_grad: float32 [80, 96], replicated
All inputs are finite; a program needn't handle non-finite values. No bound on the sum of `masks` on one device may be relied on, other than what follows from the above.
Results may differ from a plain program's by a relative error of at most 0.009.
Values may be sent and summed in bfloat16 or wider, within the bound.
A program may use at most 384 MiB of HBM per device.

v0:
```python
from functools import partial

import jax
import jax.numpy as jnp
from jax import lax
from jax.sharding import PartitionSpec as P

GROUP = 8
MICRO = 3


RHO = 0.5
CONSISTENCY = 20.0
EPSILON = 1e-05
HIGH = lax.Precision.HIGHEST


def from_behind(block, axis, distance):
    devices = range(lax.axis_size(axis))
    route = [(i - distance, i) for i in devices if i - distance in devices]
    return lax.ppermute(block, axis, route)


def mish(values):
    return values * jnp.tanh(jax.nn.softplus(values))


def layer_norm(pre, gain, shift):
    centre = pre - jnp.mean(pre, axis=-1, keepdims=True)
    spread = jnp.mean(centre * centre, axis=-1, keepdims=True)
    return centre * lax.rsqrt(spread + EPSILON) * gain + shift


def norm_mish(pre, gain, shift):
    return mish(layer_norm(pre, gain, shift))


def simplex(pre):
    grouped = pre.reshape(pre.shape[0], pre.shape[1] // GROUP, GROUP)
    return jax.nn.softmax(grouped, axis=-1).reshape(pre.shape)


def tail(
    pre_next,
    logits,
    gain_three,
    shift_three,
    bins,
    fraction,
    value_bin,
    value_fraction,
    goal,
    weight,
):
    latent_next = simplex(layer_norm(pre_next, gain_three, shift_three))
    log_probs = jax.nn.log_softmax(logits, axis=-1)
    head_count = logits.shape[0]
    row_count = bins.shape[0]
    lower = jnp.concatenate(
        [bins[None], jnp.broadcast_to(value_bin[None], (head_count - 1, row_count))], axis=0
    )
    upper = jnp.concatenate(
        [fraction[None], jnp.broadcast_to(value_fraction[None], (head_count - 1, row_count))],
        axis=0,
    )
    columns = lax.broadcasted_iota(jnp.int32, logits.shape, 2)
    two_hot = jnp.where(columns == lower[:, :, None], 1.0 - upper[:, :, None], 0.0)
    two_hot = two_hot + jnp.where(columns == lower[:, :, None] + 1, upper[:, :, None], 0.0)
    cross = -jnp.sum(two_hot * log_probs, axis=-1)
    head_index = lax.broadcasted_iota(jnp.int32, (head_count, 1), 0)
    head_weight = jnp.where(head_index == 0, 1.0, 1.0 / (head_count - 1))
    cross_total = jnp.sum(cross * head_weight, axis=0)
    differ = latent_next - goal
    consist = CONSISTENCY * jnp.mean(differ * differ, axis=-1)
    return (latent_next, jnp.sum(weight * (cross_total + consist)))


def matmul(form, left, right):
    return jnp.einsum(form, left, right, preferred_element_type=jnp.float32)


def on_device(
    latents,
    actions,
    tasks,
    masks,
    reward_bins,
    reward_frac,
    value_bins,
    value_frac,
    targets,
    task_table,
    w_latent,
    w_action,
    w_task,
    gain_one,
    shift_one,
    w_hidden,
    gain_two,
    shift_two,
    w_next,
    bias_next,
    gain_three,
    shift_three,
    w_head,
    bias_head,
):
    section_index = lax.axis_index("section")
    all_rows = latents.shape[0]
    block_rows = all_rows // MICRO
    hidden_width = w_hidden.shape[-1]
    branches = w_hidden.shape[1]
    total_rows = all_rows * lax.axis_size("batch")
    rho_power = jnp.where(section_index == 0, 1.0, RHO).astype(jnp.float32)
    latent_w = w_latent[0]
    action_w = w_action[0]
    task_w = w_task[0]
    gains_one = gain_one[0].reshape(branches, hidden_width)
    shifts_one = shift_one[0].reshape(branches, hidden_width)
    hidden_w = w_hidden[0]
    gains_two = gain_two[0][:, None, :]
    shifts_two = shift_two[0][:, None, :]
    next_w = w_next[0]
    next_b = bias_next[0]
    gains_three = gain_three[0]
    shifts_three = shift_three[0]
    head_w = w_head[0]
    head_b = bias_head[0]
    action_rows = actions[0]
    mask_rows = masks[0]
    bin_rows = reward_bins[0]
    frac_rows = reward_frac[0]
    vbin_rows = value_bins[0]
    vfrac_rows = value_frac[0]
    goal_rows = targets[0]
    task_ids = lax.broadcasted_iota(jnp.int32, (1, task_table.shape[0]), 1)

    def conditions(offset):
        acts = lax.dynamic_slice_in_dim(action_rows, offset, block_rows, 0)
        id_rows = lax.dynamic_slice_in_dim(tasks, offset, block_rows, 0)
        one_hot = (id_rows[:, None] == task_ids).astype(jnp.bfloat16)
        embedded = matmul("rt,te->re", one_hot, task_table).astype(jnp.bfloat16)
        return (acts, one_hot, embedded)

    def place(buffer, piece, offset, valid):
        older = lax.dynamic_slice_in_dim(buffer, offset, block_rows, 0)
        return lax.dynamic_update_slice_in_dim(buffer, jnp.where(valid, piece, older), offset, 0)

    received = jnp.zeros((block_rows, latents.shape[1]), jnp.bfloat16)
    kept_inputs = jnp.zeros_like(latents)
    for moment in range(MICRO + 1):
        micro_index = moment - section_index
        valid = (micro_index >= 0) & (micro_index < MICRO)
        offset = jnp.clip(micro_index, 0, MICRO - 1) * block_rows
        own_rows = lax.dynamic_slice_in_dim(latents, offset, block_rows, 0)
        latent_in = jnp.where(section_index == 0, own_rows, received)
        kept_inputs = place(kept_inputs, latent_in, offset, valid)
        if moment < MICRO:
            acts, one_hot, embedded = conditions(offset)
            pre_one = (
                matmul("rl,lh->rh", latent_in, latent_w[:, :hidden_width])
                + matmul("ra,ah->rh", acts, action_w[:, :hidden_width])
                + matmul("re,eh->rh", embedded, task_w[:, :hidden_width])
            )
            hidden_one = norm_mish(pre_one, gains_one[0], shifts_one[0]).astype(jnp.bfloat16)
            pre_two = matmul("rh,hj->rj", hidden_one, hidden_w[0])
            hidden_two = norm_mish(pre_two, gains_two[0], shifts_two[0]).astype(jnp.bfloat16)
            pre_next = matmul("rh,hl->rl", hidden_two, next_w) + next_b
            sent = simplex(layer_norm(pre_next, gains_three, shifts_three)).astype(jnp.bfloat16)
            received = from_behind(sent, "section", 1)
    grad_received = jnp.zeros((block_rows, latents.shape[1]), jnp.bfloat16)
    outputs_next = jnp.zeros_like(latents)
    input_grads = jnp.zeros_like(latents)
    loss_sum = jnp.float32(0.0)
    head_b_grad = jnp.zeros(head_b.shape, jnp.float32)
    table_grads = jnp.zeros(task_table.shape, jnp.float32)
    sums = None
    for moment in range(MICRO + 1):
        micro_index = moment - 1 + section_index
        valid = (micro_index >= 0) & (micro_index < MICRO)
        offset = jnp.clip(micro_index, 0, MICRO - 1) * block_rows
        latent_in = lax.dynamic_slice_in_dim(kept_inputs, offset, block_rows, 0)
        acts, one_hot, embedded = conditions(offset)
        mask_piece = lax.dynamic_slice_in_dim(mask_rows, offset, block_rows, 0)
        bins = lax.dynamic_slice_in_dim(bin_rows, offset, block_rows, 0)
        fraction = lax.dynamic_slice_in_dim(frac_rows, offset, block_rows, 0)
        value_bin = lax.dynamic_slice_in_dim(vbin_rows, offset, block_rows, 0)
        value_fraction = lax.dynamic_slice_in_dim(vfrac_rows, offset, block_rows, 0)
        goal = lax.dynamic_slice_in_dim(goal_rows, offset, block_rows, 0).astype(jnp.float32)
        weight = rho_power * mask_piece.astype(jnp.float32) * valid.astype(jnp.float32)
        upstream = jnp.where(valid & (section_index == 0), grad_received.astype(jnp.float32), 0.0)
        pre_one = (
            matmul("rl,lh->rh", latent_in, latent_w)
            + matmul("ra,ah->rh", acts, action_w)
            + matmul("re,eh->rh", embedded, task_w)
        )
        hidden_one, back_one = jax.vjp(
            norm_mish, pre_one.reshape(block_rows, branches, hidden_width), gains_one, shifts_one
        )
        hidden_one = hidden_one.astype(jnp.bfloat16)
        pre_two = matmul("rkh,khj->krj", hidden_one, hidden_w)
        hidden_two, back_two = jax.vjp(norm_mish, pre_two, gains_two, shifts_two)
        hidden_two = hidden_two.astype(jnp.bfloat16)
        pre_next = matmul("rh,hl->rl", hidden_two[0], next_w) + next_b
        logits = matmul("krh,khb->krb", hidden_two[1:], head_w) + head_b[:, None, :]
        (latent_next, loss_part), back_tail = jax.vjp(
            partial(
                tail,
                bins=bins,
                fraction=fraction,
                value_bin=value_bin,
                value_fraction=value_fraction,
                goal=goal,
                weight=weight,
            ),
            pre_next,
            logits,
            gains_three,
            shifts_three,
        )
        d_next, d_logits, d_gains_three, d_shifts_three = back_tail((upstream, jnp.float32(1.0)))
        d_next = d_next.astype(jnp.bfloat16)
        d_logits = d_logits.astype(jnp.bfloat16)
        fresh_next_w = matmul("rh,rl->hl", hidden_two[0], d_next)
        fresh_next_b = jnp.sum(d_next.astype(jnp.float32), axis=0)
        fresh_head_w = matmul("krh,krb->khb", hidden_two[1:], d_logits)
        head_b_grad = head_b_grad + jnp.sum(d_logits.astype(jnp.float32), axis=1)
        d_hidden_two = jnp.concatenate(
            [matmul("rl,hl->rh", d_next, next_w)[None], matmul("krb,khb->krh", d_logits, head_w)],
            axis=0,
        )
        d_two, d_gains_two, d_shifts_two = back_two(d_hidden_two)
        d_two = d_two.astype(jnp.bfloat16)
        fresh_hidden_w = matmul("rkh,krj->khj", hidden_one, d_two)
        d_hidden_one = matmul("krj,khj->rkh", d_two, hidden_w)
        d_one, d_gains_one, d_shifts_one = back_one(d_hidden_one)
        d_one = d_one.reshape(block_rows, branches * hidden_width).astype(jnp.bfloat16)
        fresh_latent_w = matmul("rl,rh->lh", latent_in, d_one)
        fresh_action_w = matmul("ra,rh->ah", acts, d_one)
        fresh_task_w = matmul("re,rh->eh", embedded, d_one)
        d_latent = matmul("rh,lh->rl", d_one, latent_w).astype(jnp.bfloat16)
        d_embedded = matmul("rh,eh->re", d_one, task_w)
        table_grads = table_grads + jnp.einsum(
            "rt,re->te", one_hot.astype(jnp.float32), d_embedded, precision=HIGH
        )
        loss_sum = loss_sum + loss_part
        outputs_next = place(outputs_next, latent_next.astype(jnp.bfloat16), offset, valid)
        input_grads = place(input_grads, d_latent, offset, valid)
        if moment < MICRO:
            grad_received = from_behind(d_latent, "section", -1)
        fresh = (
            fresh_latent_w,
            fresh_action_w,
            fresh_task_w,
            d_gains_one.reshape(-1),
            d_shifts_one.reshape(-1),
            fresh_hidden_w,
            d_gains_two.reshape(branches, hidden_width),
            d_shifts_two.reshape(branches, hidden_width),
            fresh_next_w,
            fresh_next_b,
            d_gains_three,
            d_shifts_three,
            fresh_head_w,
        )
        if sums is None:
            sums = fresh
        else:
            sums = tuple((older + newer for older, newer in zip(sums, fresh)))
    sums = (
        lax.psum_scatter(sums[0], "batch", scatter_dimension=1, tiled=True),
        lax.psum_scatter(sums[1], "batch", scatter_dimension=1, tiled=True),
        lax.psum_scatter(sums[2], "batch", scatter_dimension=1, tiled=True),
        lax.psum_scatter(sums[3], "batch", scatter_dimension=0, tiled=True),
        lax.psum_scatter(sums[4], "batch", scatter_dimension=0, tiled=True),
        lax.psum_scatter(sums[5], "batch", scatter_dimension=2, tiled=True),
        lax.psum_scatter(sums[6], "batch", scatter_dimension=1, tiled=True),
        lax.psum_scatter(sums[7], "batch", scatter_dimension=1, tiled=True),
        lax.psum_scatter(sums[8], "batch", scatter_dimension=0, tiled=True),
        lax.psum_scatter(sums[9], "batch", scatter_dimension=0, tiled=True),
        lax.psum_scatter(sums[10], "batch", scatter_dimension=0, tiled=True),
        lax.psum_scatter(sums[11], "batch", scatter_dimension=0, tiled=True),
        lax.psum_scatter(sums[12], "batch", scatter_dimension=1, tiled=True),
    )
    head_b_total, loss_total = lax.psum((head_b_grad, loss_sum), "batch")
    table_total = lax.psum(table_grads, ("section", "batch"))
    scale = 1.0 / total_rows
    scaled = tuple(((g * scale)[None] for g in sums))
    return (
        outputs_next[None],
        input_grads[None],
        (loss_total * scale).reshape(1),
        scaled[0],
        scaled[1],
        scaled[2],
        scaled[3],
        scaled[4],
        scaled[5],
        scaled[6],
        scaled[7],
        scaled[8],
        scaled[9],
        scaled[10],
        scaled[11],
        scaled[12],
        (head_b_total * scale)[None],
        table_total * scale,
    )


def solution(mesh):
    in_specs = (
        P("batch", None),
        P("section", "batch", None),
        P("batch"),
        P("section", "batch"),
        P("section", "batch"),
        P("section", "batch"),
        P("section", "batch"),
        P("section", "batch"),
        P("section", "batch", None),
        P(),
        P("section", None, None),
        P("section", None, None),
        P("section", None, None),
        P("section", None),
        P("section", None),
        P("section", None, None, None),
        P("section", None, None),
        P("section", None, None),
        P("section", None, None),
        P("section", None),
        P("section", None),
        P("section", None),
        P("section", None, None, None),
        P("section", None, None),
    )
    out_specs = (
        P("section", "batch", None),
        P("section", "batch", None),
        P("section"),
        P("section", None, "batch"),
        P("section", None, "batch"),
        P("section", None, "batch"),
        P("section", "batch"),
        P("section", "batch"),
        P("section", None, None, "batch"),
        P("section", None, "batch"),
        P("section", None, "batch"),
        P("section", "batch", None),
        P("section", "batch"),
        P("section", "batch"),
        P("section", "batch"),
        P("section", None, "batch", None),
        P("section", None, None),
        P(),
    )
    return jax.shard_map(
        on_device, mesh=mesh, in_specs=in_specs, out_specs=out_specs, check_vma=False
    )
```

profile of v0, /device:TPU:0, one launch (start us, length us, event | category | flops | bytes accessed | tf_op | source)
XLA Modules:
  0.0 1626.9 jit_solution(6167089446909716946)
XLA Ops:
  29.6 6.0 collective-permute-start
  126.1 4.3 collective-permute-start.2
  136.9 7.3 convolution_add_fusion.7
  148.4 8.6 copy.118
  157.0 8.2 copy.119
  168.7 7.4 convolution_add_fusion.6
  180.2 8.4 copy.123
  192.1 8.3 copy.124
  200.3 7.3 convolution_add_fusion.5
  211.8 8.4 copy.128
  223.6 8.2 copy.129
  231.9 7.3 convolution_add_fusion.4
  243.4 8.4 copy.133
  255.3 8.7 copy.134
  279.0 16.1 fusion.441
  295.2 17.8 %fusion.440 = (f32[7,256]{1,0:T(8,128)S(1)}, f32[7,256,1024]{2,1,0:T(8,128)}) fusion(bf16[1,7,1024,1024]{3,2,1,0:T(8,128)(2,1)} %param.42, f32[256,7,1024]{2,0,1:T(8,128)} %copy.129, f32[256,7]{0,1:T(8,128)S(1)} %fusion.319, f32[256,7]{0,1:T(8,128)S(1)} %broadcast_multiply_fusion.6, f32[7,1024]{1,0:T(8,128)S(1)} %add.883, f32[7,1024]{1,0:T(8,128)S(1)} %mul.1408), kind=kOutput, calls=%fused_computation.831 | convolution fusion | flops 3781949696 | bytes 29438976 | tf_op jit(solution)/shard_map/rkh,khj->krj/dot_general | solution.py:79
  313.1 16.1 fusion.439
  329.3 16.2 fusion.438
  346.4 4.3 multiply_reduce_fusion.18
  356.4 24.9 %fusion.82 = (bf16[7,256,1024]{2,1,0:T(8,128)(2,1)S(1)}, bf16[7,256,1024]{2,1,0:T(8,128)(2,1)S(1)}, bf16[7,256,1024]{2,1,0:T(8,128)(2,1)S(1)}, bf16[7,256,1024]{2,1,0:T(8,128)(2,1)S(1)}) fusion(f32[7,256,1024]{2,1,0:T(8,128)} %get-tuple-element.329, f32[7,1024]{1,0:T(8,128)S(1)} %copy-done.64, f32[7,1024]{1,0:T(8,128)S(1)} %copy-done.50, ...), kind=kLoop, calls=%fused_computation.166 | loop fusion | flops 88080384 | bytes 44154880 | tf_op jit(solution)/shard_map/convert_element_type | solution.py:203
  467.9 4.8 multiply_reduce_fusion.34
  493.1 13.2 multiply_reduce_fusion.3
  510.6 26.3 %fusion.405 = (f32[7,1024]{1,0:T(8,128)}, f32[256,7]{0,1:T(8,128)S(1)}, f32[256,7,1024]{2,0,1:T(8,128)}) fusion(f32[7,1024]{1,0:T(8,128)S(1)} %mul.1408, f32[256,7,1024]{2,0,1:T(8,128)} %copy.119, f32[256,7]{0,1:T(8,128)S(1)} %broadcast_multiply_fusion.8, f32[7,1024]{1,0:T(8,128)S(1)} %add.883, f32[256,7]{0,1:T(8,128)S(1)} %fusion.315, ...), kind=kOutput, calls=%fused_computation.808 | convolution fusion | flops 3811302656 | bytes 36814848 | tf_op jit(solution)/shard_map/krj,khj->rkh/dot_general | solution.py:79
  536.9 7.5 multiply_reduce_fusion.7
  544.4 5.7 add_convert_fusion.6
  550.0 6.3 copy.141
  560.5 7.1 select_dynamic-update-slice_fusion.2
  570.9 5.1 collective-permute-done.3
  588.5 14.3 multiply_reduce_fusion.2
  602.8 4.3 fusion.421
  607.1 26.3 %fusion.404 = (f32[7,1024]{1,0:T(8,128)}, f32[256,7]{0,1:T(8,128)S(1)}, f32[256,7,1024]{2,0,1:T(8,128)}) fusion(f32[7,1024]{1,0:T(8,128)S(1)} %mul.1408, f32[256,7,1024]{2,0,1:T(8,128)} %copy.124, f32[256,7]{0,1:T(8,128)S(1)} %copy-done.81, f32[7,1024]{1,0:T(8,128)S(1)} %add.883, f32[256,7]{0,1:T(8,128)S(1)} %copy-done.102, ...), kind=kOutput, calls=%fused_computation.807 | convolution fusion | flops 3811302656 | bytes 36814848 | tf_op jit(solution)/shard_map/krj,khj->rkh/dot_general | solution.py:79
  633.4 7.5 multiply_reduce_fusion.6
  640.8 5.6 add_convert_fusion.4
  646.5 6.5 copy.145
  653.0 7.1 select_dynamic-update-slice_fusion.1
  663.4 5.2 collective-permute-done.4
  679.1 14.1 multiply_reduce_fusion.1
  697.5 26.2 %fusion.406 = (f32[7,1024]{1,0:T(8,128)}, f32[256,7]{0,1:T(8,128)S(1)}, f32[256,7,1024]{2,0,1:T(8,128)}) fusion(f32[7,1024]{1,0:T(8,128)S(1)} %mul.1408, f32[256,7,1024]{2,0,1:T(8,128)} %copy.129, f32[256,7]{0,1:T(8,128)S(1)} %copy-done.78, f32[7,1024]{1,0:T(8,128)S(1)} %add.883, f32[256,7]{0,1:T(8,128)S(1)} %copy-done.99, ...), kind=kOutput, calls=%fused_computation.809 | convolution fusion | flops 3811302656 | bytes 36814848 | tf_op jit(solution)/shard_map/krj,khj->rkh/dot_general | solution.py:79
  723.8 7.5 multiply_reduce_fusion.5
  731.3 5.7 add_convert_fusion.2
  737.0 6.7 copy.149
  743.8 7.1 select_dynamic-update-slice_fusion
  753.4 5.9 collective-permute-done.5
  769.7 13.5 multiply_reduce_fusion
  788.7 26.4 %fusion.407 = (f32[7,1024]{1,0:T(8,128)}, f32[256,7]{0,1:T(8,128)S(1)}, f32[256,7,1024]{2,0,1:T(8,128)}) fusion(f32[7,1024]{1,0:T(8,128)S(1)} %mul.1408, f32[256,7,1024]{2,0,1:T(8,128)} %copy.134, f32[256,7]{0,1:T(8,128)S(1)} %copy-done.68, f32[7,1024]{1,0:T(8,128)S(1)} %add.883, f32[256,7]{0,1:T(8,128)S(1)} %copy-done.71, ...), kind=kOutput, calls=%fused_computation.810 | convolution fusion | flops 3811302656 | bytes 36814848 | tf_op jit(solution)/shard_map/krj,khj->rkh/dot_general | solution.py:79
  815.2 7.5 multiply_reduce_fusion.4
  822.7 5.7 add_convert_fusion
  829.5 6.3 copy.153
  841.5 7.7 add_add_fusion.10
  865.9 4.8 copy.175
  870.8 9.5 fusion.261
  880.3 8.4 fusion.258
  888.7 8.4 fusion.255
  897.1 20.7 %add_add_fusion.1 = f32[512,7168]{0,1:T(8,128)} fusion(f32[512,7168]{0,1:T(8,128)} %fusion.255, f32[512,7168]{0,1:T(8,128)} %fusion.261, f32[512,7168]{0,1:T(8,128)} %fusion.258, bf16[256,7168]{0,1:T(8,128)(2,1)S(1)} %bitcast.581, bf16[768,512]{1,0:T(8,128)(2,1)} %select_dynamic-update-slice_fusion.6, s32[]{:T(128)S(6)} %select_n.315), kind=kOutput, calls=%fused_computation.48 | convolution fusion | flops 1890058240 | bytes 62652420 | tf_op jit(solution)/shard_map/rl,rh->lh/dot_general | solution.py:79
  918.5 19.3 %fusion.92 = f32[7,1024,1024]{1,2,0:T(8,128)} fusion(f32[7,256,1024]{2,1,0:T(8,128)} %get-tuple-element.234, f32[7,256]{1,0:T(8,128)S(1)} %copy-done.109, f32[256,7,1024]{2,0,1:T(8,128)} %copy.119, f32[7,1024]{1,0:T(8,128)S(1)} %add.883, f32[7,1024]{1,0:T(8,128)S(1)} %mul.1408, f32[256,7]{0,1:T(8,128)S(1)} %copy-done.105, f32[256,7]{0,1:T(8,128)S(1)} %copy-done.84), kind=kOutput, calls=%fused_computation.201 | convolution fusion | flops 3783786496 | bytes 44119040 | tf_op jit(solution)/shard_map/rkh,krj->khj/dot_general | solution.py:79
  937.9 18.6 %fusion.93 = f32[7,1024,1024]{1,2,0:T(8,128)} fusion(f32[7,256,1024]{2,1,0:T(8,128)} %get-tuple-element.227, f32[7,256]{1,0:T(8,128)S(1)} %copy-done.111, f32[256,7,1024]{2,0,1:T(8,128)} %copy.124, f32[256,7]{0,1:T(8,128)S(1)} %copy-done.103, f32[256,7]{0,1:T(8,128)S(1)} %copy-done.82, f32[7,1024]{1,0:T(8,128)S(1)} %add.883, f32[7,1024]{1,0:T(8,128)S(1)} %mul.1408), kind=kOutput, calls=%fused_computation.202 | convolution fusion | flops 3783786496 | bytes 44119040 | tf_op jit(solution)/shard_map/rkh,krj->khj/dot_general | solution.py:79
  956.5 18.8 %fusion.94 = f32[7,1024,1024]{1,2,0:T(8,128)} fusion(f32[7,256,1024]{2,1,0:T(8,128)} %get-tuple-element.220, f32[7,256]{1,0:T(8,128)S(1)} %copy-done.113, f32[256,7,1024]{2,0,1:T(8,128)} %copy.129, f32[256,7]{0,1:T(8,128)S(1)} %copy-done.100, f32[256,7]{0,1:T(8,128)S(1)} %copy-done.79, f32[7,1024]{1,0:T(8,128)S(1)} %add.883, f32[7,1024]{1,0:T(8,128)S(1)} %mul.1408), kind=kOutput, calls=%fused_computation.203 | convolution fusion | flops 3783786496 | bytes 44119040 | tf_op jit(solution)/shard_map/rkh,krj->khj/dot_general | solution.py:79
  975.3 47.0 %add_add_fusion = f32[7,1024,1024]{1,2,0:T(8,128)} fusion(f32[7,1024,1024]{1,2,0:T(8,128)} %fusion.94, f32[7,1024,1024]{1,2,0:T(8,128)} %fusion.92, f32[7,1024,1024]{1,2,0:T(8,128)} %fusion.93, f32[7,256,1024]{2,1,0:T(8,128)} %get-tuple-element.213, f32[7,256]{1,0:T(8,128)S(1)} %copy-done.86, f32[256,7,1024]{2,0,1:T(8,128)} %copy.134, ...), kind=kOutput, calls=%fused_computation.7 | convolution fusion | flops 3805806592 | bytes 132199424 | tf_op jit(solution)/shard_map/rkh,krj->khj/dot_general | solution.py:79
  1040.7 59.6 %all-reduce.7 = (f32[]{:T(128)}, f32[7168]{0:T(1024)S(1)}, f32[7168]{0:T(1024)S(1)}, f32[512]{0:T(512)S(1)}, f32[512]{0:T(512)S(1)}, /*index=5*/f32[512]{0:T(512)S(1)}, f32[6,101]{1,0:T(8,128)S(1)}) all-reduce(f32[]{:T(128)S(6)} %add.953, f32[7168]{0:T(1024)S(1)} %add.966, ...), channel_id=1, replica_groups=mesh['section'=2,'batch'=16] {'batch'}, use_global_device_ids=true, to_apply=%region_106.110 | all-reduce | flops 16479 | bytes 131832 | tf_op jit(solution)/shard_map/psum | solution.py:285
  1104.7 37.5 %psum.23 = f32[80,96]{1,0:T(8,128)S(1)} all-reduce(f32[80,96]{1,0:T(8,128)S(1)} %convolution_add_fusion.25), channel_id=1, replica_groups=mesh['section'=2,'batch'=16] {'section','batch'}, use_global_device_ids=true, to_apply=%region_153.157 | all-reduce | flops 7680 | bytes 61440 | tf_op jit(solution)/shard_map/psum | solution.py:286
  1145.8 6.3 fusion.134
  1159.9 21.1 %reduce-scatter.27.cloned.1.call-done = f32[448,96]{1,0:T(8,128)} async-done(((f32[7168,96]{1,0:T(8,128)}), f32[448,96]{1,0:T(8,128)}) %reduce-scatter.27.cloned.1.call-update) | async-done | bytes 172048
  1182.8 151.3 %reduce-scatter.17.cloned.1.call-done = f32[512,448]{0,1:T(8,128)} async-done(((f32[512,7168]{0,1:T(8,128)}), f32[512,448]{0,1:T(8,128)}) %reduce-scatter.17.cloned.1.call-update) | async-done | bytes 917520 | tf_op jit(solution)/shard_map/reduce_scatter | solution.py:271
  1336.3 279.4 %reduce-scatter.19.cloned.1.call-done = f32[7,1024,64]{1,2,0:T(8,128)} async-done(((f32[7,1024,1024]{1,2,0:T(8,128)}), f32[7,1024,64]{1,2,0:T(8,128)}) %reduce-scatter.19.cloned.1.call-update) | async-done | bytes 1835024 | tf_op jit(solution)/shard_map/reduce_scatter | solution.py:276
  (930 shorter events, 396.9 us)
Async XLA Ops:
  7.2 375.3 %copy-start = (bf16[1,6,1024,101]{2,3,1,0:T(8,128)(2,1)S(1)}, bf16[1,6,1024,101]{2,3,1,0:T(8,128)(2,1)}, u32[]{:S(2)}) copy-start(bf16[1,6,1024,101]{2,3,1,0:T(8,128)(2,1)} %param.49) | copy-start | bytes 3723268
  7.2 1144.9 %reduce-scatter.29.cloned.1.call-start = ((), (), s32[]{:S(2)}) async-start(), calls=%async_computation.14 | async-start | bytes 557056
  29.6 48.7 %collective-permute-start = (bf16[256,512]{1,0:T(8,128)(2,1)}, bf16[256,512]{1,0:T(8,128)(2,1)}, u32[]{:S(2)}, u32[]{:S(2)}) collective-permute-start(bf16[256,512]{1,0:T(8,128)(2,1)} %divide_convert_fusion.2), channel_id=1, source_target_pairs={{0,16},{1,17},{2,18},{3,19},{4,20},{5,21},{6,22},{7,23},{8,24},{9,... | collective-permute-start | bytes 786440 | tf_op jit(solution)/shard_map/ppermute | solution.py:21
  48.5 27.4 %copy-start.12 = (bf16[1,96,7168]{2,1,0:T(8,128)(2,1)S(1)}, bf16[1,96,7168]{2,1,0:T(8,128)(2,1)}, u32[]{:S(2)}) copy-start(bf16[1,96,7168]{2,1,0:T(8,128)(2,1)} %param.39) | copy-start | bytes 4128772
  63.7 175.5 %copy-start.90 = (bf16[256,96]{0,1:T(8,128)(2,1)}, bf16[256,96]{0,1:T(8,128)(2,1)S(1)}, u32[]{:S(2)}) copy-start(bf16[256,96]{0,1:T(8,128)(2,1)S(1)} %convolution_convert_fusion.4) | copy-start | bytes 147460
  64.7 142.9 %copy-start.92 = (bf16[256,96]{0,1:T(8,128)(2,1)}, bf16[256,96]{0,1:T(8,128)(2,1)S(1)}, u32[]{:S(2)}) copy-start(bf16[256,96]{0,1:T(8,128)(2,1)S(1)} %convolution_convert_fusion.5) | copy-start | bytes 147460
  86.7 22.3 %copy-start.239 = (f32[1,1024]{1,0:T(1,128)S(1)}, f32[1,1024]{1,0:T(1,128)}, u32[]{:S(2)}) copy-start(f32[1,1024]{1,0:T(1,128)} %copy-done.238) | copy-start | bytes 12292
  86.7 22.3 %copy-start.241 = (f32[1,1024]{1,0:T(1,128)S(1)}, f32[1,1024]{1,0:T(1,128)}, u32[]{:S(2)}) copy-start(f32[1,1024]{1,0:T(1,128)} %copy-done.240) | copy-start | bytes 12292
  99.0 7.1 collective-permute-start.1
  126.1 9.0 collective-permute-start.2
  264.0 280.3 %copy-start.83 = (f32[256,7]{0,1:T(8,128)}, f32[256,7]{0,1:T(8,128)S(1)}, u32[]{:S(2)}) copy-start(f32[256,7]{0,1:T(8,128)S(1)} %broadcast_multiply_fusion.8) | copy-start | bytes 21508
  268.8 275.6 %copy-start.104 = (f32[256,7]{0,1:T(8,128)}, f32[256,7]{0,1:T(8,128)S(1)}, u32[]{:S(2)}) copy-start(f32[256,7]{0,1:T(8,128)S(1)} %fusion.315) | copy-start | bytes 21508
  268.8 44.3 %copy-start.80 = (f32[256,7]{0,1:T(8,128)}, f32[256,7]{0,1:T(8,128)S(1)}, u32[]{:S(2)}) copy-start(f32[256,7]{0,1:T(8,128)S(1)} %broadcast_multiply_fusion.7) | copy-start | bytes 21508
  272.9 40.1 %copy-start.101 = (f32[256,7]{0,1:T(8,128)}, f32[256,7]{0,1:T(8,128)S(1)}, u32[]{:S(2)}) copy-start(f32[256,7]{0,1:T(8,128)S(1)} %fusion.317) | copy-start | bytes 21508
  273.5 21.7 %copy-start.77 = (f32[256,7]{0,1:T(8,128)}, f32[256,7]{0,1:T(8,128)S(1)}, u32[]{:S(2)}) copy-start(f32[256,7]{0,1:T(8,128)S(1)} %broadcast_multiply_fusion.6) | copy-start | bytes 21508
  279.0 34.1 %slice-start.2 = ((s8[7340032]{0:T(1024)(128)(4,1)}), s8[4194304]{0:T(1024)(128)(4,1)S(1)}, s32[]{:S(2)}) async-start(s8[7340032]{0:T(1024)(128)(4,1)} %bitcast.570), calls=%async_computation.18 | async-start | bytes 8388608
  295.2 61.1 %copy-start.114 = (f32[7,256]{1,0:T(8,128)}, f32[7,256]{1,0:T(8,128)S(1)}, u32[]{:S(2)}) copy-start(f32[7,256]{1,0:T(8,128)S(1)} %broadcast_multiply_fusion.1) | copy-start | bytes 21508
  295.2 34.0 %slice-start = ((s8[7340032]{0:T(1024)(128)(4,1)}), s8[4194304]{0:T(1024)(128)(4,1)S(1)}, s32[]{:S(2)}) async-start(s8[7340032]{0:T(1024)(128)(4,1)} %bitcast.568), calls=%async_computation.16 | async-start | bytes 8388608
  313.1 43.2 %copy-start.116 = (f32[7,256]{1,0:T(8,128)}, f32[7,256]{1,0:T(8,128)S(1)}, u32[]{:S(2)}) copy-start(f32[7,256]{1,0:T(8,128)S(1)} %broadcast_multiply_fusion.2) | copy-start | bytes 21508
  313.1 32.4 %slice-start.6 = ((s8[7340032]{0:T(1024)(128)(4,1)}), s8[3145728]{0:T(1024)(128)(4,1)S(1)}, s32[]{:S(2)}) async-start(s8[7340032]{0:T(1024)(128)(4,1)} %bitcast.582), calls=%async_computation.22 | async-start | bytes 6291456
  352.3 29.1 %copy-start.170 = (f32[7,256]{1,0:T(8,128)}, f32[7,256]{1,0:T(8,128)S(1)}, u32[]{:S(2)}) copy-start(f32[7,256]{1,0:T(8,128)S(1)} %multiply_reduce_fusion.20) | copy-start | bytes 21508
  356.3 25.1 %copy-start.172 = (f32[7,256]{1,0:T(8,128)}, f32[7,256]{1,0:T(8,128)S(1)}, u32[]{:S(2)}) copy-start(f32[7,256]{1,0:T(8,128)S(1)} %multiply_reduce_fusion.22) | copy-start | bytes 21508
  356.4 25.0 %copy-start.28 = (bf16[1,1024,512]{2,1,0:T(8,128)(2,1)S(1)}, bf16[1,1024,512]{2,1,0:T(8,128)(2,1)}, u32[]{:S(2)}) copy-start(bf16[1,1024,512]{2,1,0:T(8,128)(2,1)} %param.45) | copy-start | bytes 3145732
  356.4 25.0 %copy-start.250 = (f32[1,512]{1,0:T(1,128)S(1)}, f32[1,512]{1,0:T(1,128)}, u32[]{:S(2)}) copy-start(f32[1,512]{1,0:T(1,128)} %param.46) | copy-start | bytes 6148
  356.4 26.1 %copy-start.53 = (f32[1,6,101]{2,1,0:T(8,128)S(1)}, f32[1,6,101]{2,1,0:T(8,128)}, u32[]{:S(2)}) copy-start(f32[1,6,101]{2,1,0:T(8,128)} %copy.187) | copy-start | bytes 7276
  392.5 20.3 %copy-start.185 = (f32[256]{0:T(256)}, f32[256]{0:T(256)S(1)}, u32[]{:S(2)}) copy-start(f32[256]{0:T(256)S(1)} %broadcast_multiply_fusion.16) | copy-start | bytes 3076
  394.8 21.0 %copy-start.148 = (f32[6,256]{1,0:T(8,128)S(1)}, f32[6,256]{1,0:T(8,128)}, u32[]{:S(2)}) copy-start(f32[6,256]{1,0:T(8,128)} %get-tuple-element.261) | copy-start | bytes 18436
  394.8 21.0 %copy-start.149 = (f32[6,256]{1,0:T(8,128)S(1)}, f32[6,256]{1,0:T(8,128)}, u32[]{:S(2)}) copy-start(f32[6,256]{1,0:T(8,128)} %get-tuple-element.262) | copy-start | bytes 18436
  394.8 21.0 %copy-start.150 = (s32[6,256]{1,0:T(8,128)S(1)}, s32[6,256]{1,0:T(8,128)}, u32[]{:S(2)}) copy-start(s32[6,256]{1,0:T(8,128)} %get-tuple-element.358) | copy-start | bytes 18436
  394.8 21.0 %copy-start.151 = (s32[6,256]{1,0:T(8,128)S(1)}, s32[6,256]{1,0:T(8,128)}, u32[]{:S(2)}) copy-start(s32[6,256]{1,0:T(8,128)} %get-tuple-element.359) | copy-start | bytes 18436
  394.8 21.0 %copy-start.157 = (f32[6,256]{1,0:T(8,128)S(1)}, f32[6,256]{1,0:T(8,128)}, u32[]{:S(2)}) copy-start(f32[6,256]{1,0:T(8,128)} %get-tuple-element.307) | copy-start | bytes 18436
  396.0 71.9 %copy-start.30 = (f32[256,512]{1,0:T(8,128)}, f32[256,512]{1,0:T(8,128)S(1)}, u32[]{:S(2)}) copy-start(f32[256,512]{1,0:T(8,128)S(1)} %get-tuple-element.270) | copy-start | bytes 1572868
  396.0 71.9 %copy-start.32 = (f32[256,512]{1,0:T(8,128)}, f32[256,512]{1,0:T(8,128)S(1)}, u32[]{:S(2)}) copy-start(f32[256,512]{1,0:T(8,128)S(1)} %get-tuple-element.268) | copy-start | bytes 1572868
  442.8 23.8 %copy-start.247 = (f32[6]{0:T(128)S(1)}, f32[6]{0:T(128)}, u32[]{:S(2)}) copy-start(f32[6]{0:T(128)} %compare_select_fusion.30) | copy-start | bytes 76
  445.3 43.9 %copy-start.51 = (bf16[6,256,101]{1,2,0:T(8,128)(2,1)}, bf16[6,256,101]{1,2,0:T(8,128)(2,1)S(1)}, u32[]{:S(2)}) copy-start(bf16[6,256,101]{1,2,0:T(8,128)(2,1)S(1)} %get-tuple-element.198) | copy-start | bytes 930820
  510.6 26.3 %copy-start.108 = (f32[7,256]{1,0:T(8,128)}, f32[7,256]{1,0:T(8,128)S(1)}, u32[]{:S(2)}) copy-start(f32[7,256]{1,0:T(8,128)S(1)} %negate_multiply_fusion.7) | copy-start | bytes 21508
  510.6 26.3 %copy-start.165 = (f32[256,7]{0,1:T(8,128)S(1)}, f32[256,7]{0,1:T(8,128)}, u32[]{:S(2)}) copy-start(f32[256,7]{0,1:T(8,128)} %copy-done.164) | copy-start | bytes 21508
  560.5 23.9 %copy-start.33 = (f32[256,512]{1,0:T(8,128)S(1)}, f32[256,512]{1,0:T(8,128)}, u32[]{:S(2)}) copy-start(f32[256,512]{1,0:T(8,128)} %copy-done.32) | copy-start | bytes 1572868
  560.5 23.9 %copy-start.41 = (f32[256,512]{1,0:T(8,128)S(1)}, f32[256,512]{1,0:T(8,128)}, u32[]{:S(2)}) copy-start(f32[256,512]{1,0:T(8,128)} %copy-done.40) | copy-start | bytes 1572868
  560.5 23.9 %copy-start.186 = (f32[256]{0:T(256)S(1)}, f32[256]{0:T(256)}, u32[]{:S(2)}) copy-start(f32[256]{0:T(256)} %copy-done.185) | copy-start | bytes 3076
  560.5 23.9 %copy-start.198 = (f32[256]{0:T(256)S(1)}, f32[256]{0:T(256)}, u32[]{:S(2)}) copy-start(f32[256]{0:T(256)} %copy-done.197) | copy-start | bytes 3076
  567.6 8.4 collective-permute-start.3
  607.1 26.3 %copy-start.110 = (f32[7,256]{1,0:T(8,128)}, f32[7,256]{1,0:T(8,128)S(1)}, u32[]{:S(2)}) copy-start(f32[7,256]{1,0:T(8,128)S(1)} %negate_multiply_fusion.5) | copy-start | bytes 21508
  607.1 26.3 %copy-start.163 = (f32[256,7]{0,1:T(8,128)S(1)}, f32[256,7]{0,1:T(8,128)}, u32[]{:S(2)}) copy-start(f32[256,7]{0,1:T(8,128)} %copy-done.162) | copy-start | bytes 21508
  653.0 19.6 %copy-start.39 = (f32[256,512]{0,1:T(8,128)S(1)}, f32[256,512]{0,1:T(8,128)}, u32[]{:S(2)}) copy-start(f32[256,512]{0,1:T(8,128)} %copy.130) | copy-start | bytes 1572868
  660.2 8.4 collective-permute-start.4
  697.5 26.2 %copy-start.112 = (f32[7,256]{1,0:T(8,128)}, f32[7,256]{1,0:T(8,128)S(1)}, u32[]{:S(2)}) copy-start(f32[7,256]{1,0:T(8,128)S(1)} %negate_multiply_fusion.3) | copy-start | bytes 21508
  697.5 26.2 %copy-start.161 = (f32[256,7]{0,1:T(8,128)S(1)}, f32[256,7]{0,1:T(8,128)}, u32[]{:S(2)}) copy-start(f32[256,7]{0,1:T(8,128)} %copy-done.160) | copy-start | bytes 21508
  750.9 8.4 collective-permute-start.5
  787.5 27.6 %copy-start.85 = (f32[7,256]{1,0:T(8,128)}, f32[7,256]{1,0:T(8,128)S(1)}, u32[]{:S(2)}) copy-start(f32[7,256]{1,0:T(8,128)S(1)} %negate_multiply_fusion.1) | copy-start | bytes 21508
  788.6 365.0 %reduce-scatter.31.cloned.1.call-start = ((), (), s32[]{:S(2)}) async-start(), calls=%async_computation.15 | async-start | bytes 557056
  788.7 26.5 %copy-start.159 = (f32[256,7]{0,1:T(8,128)S(1)}, f32[256,7]{0,1:T(8,128)}, u32[]{:S(2)}) copy-start(f32[256,7]{0,1:T(8,128)} %copy-done.158) | copy-start | bytes 21508
  835.8 319.2 %reduce-scatter.25.cloned.1.call-start = ((), (), s32[]{:S(2)}) async-start(), calls=%async_computation.12 | async-start | bytes 3899392
  841.5 315.3 %reduce-scatter.23.cloned.1.call-start = ((), (), s32[]{:S(2)}) async-start(), calls=%async_computation.11 | async-start | bytes 3342336 | tf_op jit(solution)/shard_map/reduce_scatter | solution.py:283
  849.3 309.1 %reduce-scatter.21.cloned.1.call-start = ((), (), s32[]{:S(2)}) async-start(), calls=%async_computation.10 | async-start | bytes 2228224 | tf_op jit(solution)/shard_map/reduce_scatter | solution.py:279
  856.9 324.2 %reduce-scatter.27.cloned.1.call-start = ((), (), s32[]{:S(2)}) async-start(), calls=%async_computation.13 | async-start | bytes 3899392
  870.8 463.4 %reduce-scatter.17.cloned.1.call-start = ((), (), s32[]{:S(2)}) async-start(), calls=%async_computation.8 | async-start | bytes 15597568 | tf_op jit(solution)/shard_map/reduce_scatter | solution.py:271
  917.8 20.0 %copy-start.82 = (f32[256,7]{0,1:T(8,128)S(1)}, f32[256,7]{0,1:T(8,128)}, u32[]{:S(2)}) copy-start(f32[256,7]{0,1:T(8,128)} %copy-done.80) | copy-start | bytes 21508
  917.8 20.0 %copy-start.103 = (f32[256,7]{0,1:T(8,128)S(1)}, f32[256,7]{0,1:T(8,128)}, u32[]{:S(2)}) copy-start(f32[256,7]{0,1:T(8,128)} %copy-done.101) | copy-start | bytes 21508
  917.9 20.0 %copy-start.111 = (f32[7,256]{1,0:T(8,128)S(1)}, f32[7,256]{1,0:T(8,128)}, u32[]{:S(2)}) copy-start(f32[7,256]{1,0:T(8,128)} %copy-done.110) | copy-start | bytes 21508
  917.9 697.8 %reduce-scatter.19.cloned.1.call-start = ((), (), s32[]{:S(2)}) async-start(), calls=%async_computation.9 | async-start | bytes 31195136 | tf_op jit(solution)/shard_map/reduce_scatter | solution.py:276
  1037.8 66.5 %copy-start.200 = (s32[256]{0:T(256)S(1)}, s32[256]{0:T(256)}, u32[]{:S(2)}) copy-start(s32[256]{0:T(256)} %get-tuple-element.276) | copy-start | bytes 3076
  1145.2 473.5 %copy-start.1 = (bf16[1,6,1024,101]{2,3,1,0:T(8,128)(2,1)S(1)}, bf16[1,6,1024,101]{2,3,1,0:T(8,128)(2,1)}, u32[]{:S(2)}) copy-start(bf16[1,6,1024,101]{2,3,1,0:T(8,128)(2,1)} %param.49) | copy-start | bytes 3723268
  1152.1 466.6 %copy-start.72 = (bf16[1,768,512]{2,1,0:T(8,128)(2,1)}, bf16[1,768,512]{2,1,0:T(8,128)(2,1)S(1)}, u32[]{:S(2)}) copy-start(bf16[1,768,512]{2,1,0:T(8,128)(2,1)S(1)} %fusion.134) | copy-start | bytes 2359300
  (220 other events, 2037.2 us)
Sparse Core Ops, SparseCore 0:
  788.8 56.1 reduce-scatter.28
  848.9 54.8 reduce-scatter.30
  907.6 67.6 reduce-scatter.24
  979.5 64.9 reduce-scatter.22
  1048.5 60.6 reduce-scatter.20
  1112.9 68.1 reduce-scatter.26
  1185.7 148.4 reduce-scatter.16
  1338.8 276.8 reduce-scatter.18
where the time goes:
time: 1640 us; the launch traced here: 1630 us
  matrix products  527 us (32%)
  waiting for transfers between devices  470 us (29%)
  other arithmetic  304 us (19%)
  local copies, waits for them, and re-layouts  188 us (11%)
  blocking collectives  97.1 us (6%)
  between operations  23.9 us (1%)
  starting transfers between devices  17 us (1%)
    dot_general x87, matrix products, matmul(): return jnp.einsum(form, left, right, preferred_element_type=jnp.float32)  526 us
    reduce_scatter x1, waiting for transfers between devices, on_device(): lax.psum_scatter(sums[5], 'batch', scatter_dimension=2, tiled=True)  279 us
    reduce_scatter x1, waiting for transfers between devices, on_device(): lax.psum_scatter(sums[0], 'batch', scatter_dimension=1, tiled=True)  151 us
    reduce_sum x12, other arithmetic, layer_norm(): return centre * lax.rsqrt(spread + EPSILON) * gain + shift  95.9 us
    psum x1, blocking collectives, on_device(): head_b_total, loss_total = lax.psum((head_b_grad, loss_sum), 'batch')  59.6 us
    psum x1, blocking collectives, on_device(): table_total = lax.psum(table_grads, ('section', 'batch'))  37.5 us
    add x4, local copies, waits for them, and re-layouts, on_device(): matmul('rl,lh->rh', latent_in, latent_w)  33.7 us
    reshape x4, local copies, waits for them, and re-layouts, on_device(): pre_one.reshape(block_rows, branches, hidden_width)  33.4 us
  transfers between devices with their start and end apart: 14, of which 8 were waited for; matrix products, arithmetic and copies ran while one was open for 20% of the time, Pallas kernels for 0%

commit v1 on v0

v1 whole, which is shorter than its diff:
```python
import functools

import jax
import jax.numpy as jnp
from jax import lax
from jax.experimental import pallas as pl
from jax.experimental.pallas import tpu as pltpu
from jax.sharding import PartitionSpec as P

F32 = jnp.float32
BF16 = jnp.bfloat16
GROUP = 8
RHO = 0.5
CONSISTENCY = 20.0
EPSILON = 1e-05
HIGH = lax.Precision.HIGHEST
LANES = 128
TILE = 256
CHUNK = 16
CAP = 20.0
VMEM_BYTES = 58 * 2**20


def dot(left, right, contract):
    return lax.dot_general(
        left, right, ((contract[:1], contract[1:]), ((), ())), preferred_element_type=F32
    )


def nn(left, right):
    return dot(left, right, (1, 0))


def nt(left, right):
    return dot(left, right, (1, 1))


def tn(left, right):
    return dot(left, right, (0, 0))


def norm_forward(pre, gain, shift, hidden, slope, unit, inverse, row):
    width = pre.shape[1]
    for start in range(0, TILE, CHUNK):
        out = slice(row + start, row + start + CHUNK)
        x = pre[start : start + CHUNK, :]
        x = x - jnp.sum(x, axis=-1, keepdims=True) * (1.0 / width)
        r = lax.rsqrt(jnp.sum(x * x, axis=-1, keepdims=True) * (1.0 / width) + EPSILON)
        if inverse is not None:
            inverse[out, :] = r
        for q in range(0, width, 256):
            cols = slice(q, q + 256)
            y = x[:, cols] * r
            v = y * gain[:, cols] + shift[:, cols]
            e = jnp.exp(jnp.minimum(v, CAP))
            k = e * (e + 2.0)
            d = 1.0 / (k + 2.0)
            t = k * d
            hidden[out, cols] = (v * t).astype(BF16)
            if slope is not None:
                slope[out, cols] = (t + (4.0 * v * d) * ((k - e) * d)).astype(BF16)
                unit[out, cols] = y.astype(BF16)


def norm_backward(grad, gain, slope, unit, inverse, result, gain_sum, shift_sum, row):
    width = grad.shape[1]
    gains = shifts = None
    for start in range(0, TILE, CHUNK):
        out = slice(row + start, row + start + CHUNK)
        y = unit[out, :].astype(F32)
        dv = grad[start : start + CHUNK, :] * slope[out, :].astype(F32)
        dvy = dv * y
        g = dvy[:8] + dvy[8:]
        s = dv[:8] + dv[8:]
        gains = g if gains is None else gains + g
        shifts = s if shifts is None else shifts + s
        row_gain = gain[...]
        dx = dv * row_gain
        mean = jnp.sum(dx, axis=-1, keepdims=True) * (1.0 / width)
        along = jnp.sum(dvy * row_gain, axis=-1, keepdims=True) * (1.0 / width)
        result[out, :] = ((dx - mean - y * along) * inverse[out, :]).astype(BF16)
    gain_sum[...] += gains
    shift_sum[...] += shifts


def group_matrix():
    i = lax.broadcasted_iota(jnp.int32, (256, 256), 0) // GROUP
    j = lax.broadcasted_iota(jnp.int32, (256, 256), 1) // GROUP
    return jnp.where(i == j, 1.0, 0.0).astype(BF16)


def group_sum(values, ones):
    parts = []
    for q in range(0, values.shape[1], 256):
        v = values[:, q : q + 256]
        high = v.astype(BF16)
        low = (v - high.astype(F32)).astype(BF16)
        parts.append(nn(high, ones) + nn(low, ones))
    return jnp.concatenate(parts, axis=1)


def simplex_forward(pre, gain, shift, ones):
    width = pre.shape[1]
    x = pre - jnp.sum(pre, axis=-1, keepdims=True) * (1.0 / width)
    r = lax.rsqrt(jnp.sum(x * x, axis=-1, keepdims=True) * (1.0 / width) + EPSILON)
    y = x * r
    e = jnp.exp(y * gain + shift)
    return y, r, e / group_sum(e, ones)


def tile_rows(i):
    return slice(i * TILE, (i + 1) * TILE)


def staged(count, first, then):
    first(0)
    for i in range(count):
        if i + 1 < count:
            first(i + 1)
        then(i)


def forward_pair(x, wl, wta, g1, s1, w2, g2, s2, pre, h1, m1, x1, r1, h2, m2, x2, r2):
    count = x.shape[0] // TILE
    latent = wl.shape[0]

    def one(i):
        r = tile_rows(i)
        pre[i][...] = nn(x[r, :latent], wl[...]) + nn(x[r, latent:], wta[...])

    def two(i):
        pre[i][...] = nn(h1[tile_rows(i), :], w2[...])

    staged(count, one, lambda i: norm_forward(pre[i], g1, s1, h1, m1, x1, r1, i * TILE))
    staged(count, two, lambda i: norm_forward(pre[i], g2, s2, h2, m2, x2, r2, i * TILE))


def backward_pair(
    x, wl, wta, g1, w2, g2, pre, m1, x1, r1, m2, x2, r2, d1, d2, back_in,
    dx, add_dx, dg1, ds1, dg2, ds2,
):
    count = x.shape[0] // TILE
    latent = wl.shape[0]

    def one(i):
        pre[i][...] = nt(d2[tile_rows(i), :], w2[...])

    staged(
        count, back_in, lambda i: norm_backward(pre[i], g2, m2, x2, r2, d2, dg2, ds2, i * TILE)
    )
    staged(count, one, lambda i: norm_backward(pre[i], g1, m1, x1, r1, d1, dg1, ds1, i * TILE))
    for i in range(count):
        r = tile_rows(i)
        main, side = nt(d1[r, :], wl[...]), nt(d1[r, :], wta[...])
        if add_dx:
            dx[r, :latent] += main
            dx[r, latent:] += side
        else:
            dx[r, :latent] = main
            dx[r, latent:] = side


def weight_grads(x, h1, d1, d2, tail_left, tail_right, u):
    hidden = h1.shape[1]
    width = x.shape[1]
    for n in range(0, hidden, 256):
        cols = slice(n, n + 256)
        u[cols, :hidden] = tn(d2[:, cols], h1[...]).astype(BF16)
        u[cols, hidden : hidden + width] = tn(d1[:, cols], x[...]).astype(BF16)
        u[cols, hidden + width :] = tn(tail_left[:, cols], tail_right[...]).astype(BF16)


def heads_kernel(
    x, wl, wta, g1, s1, w2, g2, s2, wh, bh, cond,
    u, dx, head_bias, loss, small,
    p0, p1, p2, logits, h1, h2, m1, m2, x1, x2, r1, r2, d1, d2, dl,
):
    pre = (p0, p1, p2)
    w2, wh, g1, s1, g2, s2, bh, cond, u = (
        ref.at[0] for ref in (w2, wh, g1, s1, g2, s2, bh, cond, u)
    )
    sums = [small.at[0, pl.ds(8 * i, 8)] for i in range(4)]
    small[...] = jnp.zeros_like(small)
    head_bias[...] = jnp.zeros_like(head_bias)

    @pl.when(pl.program_id(0) == 0)
    def _():
        dx[...] = jnp.zeros_like(dx)
        loss[...] = jnp.zeros_like(loss)

    forward_pair(x, wl, wta, g1, s1, w2, g2, s2, pre, h1, m1, x1, r1, h2, m2, x2, r2)

    def tail(i):
        r = tile_rows(i)
        v = nn(h2[r, :], wh[...]) + bh[...]
        given = cond[r, :]
        lower, upper, weight = given[:, 0:1], given[:, 1:2], given[:, 2:3]
        v = v - jnp.max(v, axis=-1, keepdims=True)
        e = jnp.exp(v)
        total = jnp.sum(e, axis=-1, keepdims=True)
        at = lax.broadcasted_iota(jnp.int32, v.shape, 1).astype(F32)
        hot = jnp.where(at == lower, 1.0 - upper, 0.0) + jnp.where(at == lower + 1.0, upper, 0.0)
        loss[r, :] += weight * (jnp.log(total) - jnp.sum(hot * v, axis=-1, keepdims=True))
        grad = (weight * (e / total - hot)).astype(BF16)
        dl[r, :] = grad
        head_bias[0, 0:1, :] += jnp.sum(grad.astype(F32), axis=0, keepdims=True)

    for i in range(x.shape[0] // TILE):
        tail(i)

    def back_in(i):
        pre[i][...] = nt(dl[tile_rows(i), :], wh[...])

    backward_pair(
        x, wl, wta, g1, w2, g2, pre, m1, x1, r1, m2, x2, r2, d1, d2, back_in, dx, True, *sums
    )
    weight_grads(x, h1, d1, d2, h2, dl, u)


def scratch(rows, hidden, forward=False):
    def hold():
        return pltpu.VMEM((rows, hidden), BF16)

    if forward:
        return [pltpu.VMEM((TILE, hidden), F32)] * 3 + [hold(), hold()]
    return (
        [pltpu.VMEM((TILE, hidden), F32)] * 3
        + [hold() for _ in range(6)]
        + [pltpu.VMEM((rows, 1), F32)] * 2
        + [hold(), hold()]
    )


def heads(x, w_latent, wta, g1, s1, w_hidden, g2, s2, wh, bh, cond):
    rows, width = x.shape
    latent = w_latent.shape[0]
    count, hidden = wh.shape[0], w_hidden.shape[-1]
    held = scratch(rows, hidden)
    row = pl.BlockSpec((1, 1, hidden), lambda k: (k + 1, 0, 0))
    return pl.pallas_call(
        heads_kernel,
        grid=(count,),
        in_specs=[
            pl.BlockSpec((rows, width), lambda k: (0, 0)),
            pl.BlockSpec((latent, hidden), lambda k: (0, k + 1)),
            pl.BlockSpec((LANES, hidden), lambda k: (0, k + 1)),
            row,
            row,
            pl.BlockSpec((1, hidden, hidden), lambda k: (k + 1, 0, 0)),
            row,
            row,
            pl.BlockSpec((1, hidden, LANES), lambda k: (k, 0, 0)),
            pl.BlockSpec((1, 1, LANES), lambda k: (k, 0, 0)),
            pl.BlockSpec((1, rows, 8), lambda k: (jnp.minimum(k, 1), 0, 0)),
        ],
        out_shape=[
            jax.ShapeDtypeStruct((count, hidden, hidden + width + LANES), BF16),
            jax.ShapeDtypeStruct((rows, width), F32),
            jax.ShapeDtypeStruct((count, 8, LANES), F32),
            jax.ShapeDtypeStruct((rows, 1), F32),
            jax.ShapeDtypeStruct((count, 32, hidden), F32),
        ],
        out_specs=[
            pl.BlockSpec((1, hidden, hidden + width + LANES), lambda k: (k, 0, 0)),
            pl.BlockSpec((rows, width), lambda k: (0, 0)),
            pl.BlockSpec((1, 8, LANES), lambda k: (k, 0, 0)),
            pl.BlockSpec((rows, 1), lambda k: (0, 0)),
            pl.BlockSpec((1, 32, hidden), lambda k: (k, 0, 0)),
        ],
        scratch_shapes=held[:3]
        + [pltpu.VMEM((rows, LANES), F32)]
        + held[3:]
        + [pltpu.VMEM((rows, LANES), BF16)],
        compiler_params=pltpu.CompilerParams(vmem_limit_bytes=VMEM_BYTES),
    )(x, w_latent, wta, g1, s1, w_hidden, g2, s2, wh, bh, cond)


def dynamics_specs(rows, width, latent, hidden):
    row = pl.BlockSpec((1, 1, hidden), lambda k: (0, 0, 0))
    short = pl.BlockSpec((1, latent), lambda k: (0, 0))
    return [
        pl.BlockSpec((rows, width), lambda k: (0, 0)),
        pl.BlockSpec((latent, hidden), lambda k: (0, 0)),
        pl.BlockSpec((LANES, hidden), lambda k: (0, 0)),
        row,
        row,
        pl.BlockSpec((1, hidden, hidden), lambda k: (0, 0, 0)),
        row,
        row,
        pl.BlockSpec((hidden, latent), lambda k: (0, 0)),
        short,
        short,
        short,
    ]


def rollout_kernel(
    x, wl, wta, g1, s1, w2, g2, s2, wn, bn, g3, s3, z_out, p0, p1, p2, h1, h2
):
    pre = (p0, p1, p2)
    w2, g1, s1, g2, s2 = (ref.at[0] for ref in (w2, g1, s1, g2, s2))
    ones = group_matrix()
    none = (None, None, None)
    forward_pair(x, wl, wta, g1, s1, w2, g2, s2, pre, h1, *none, h2, *none)
    for i in range(x.shape[0] // TILE):
        for start in range(i * TILE, (i + 1) * TILE, 64):
            r = slice(start, start + 64)
            v = nn(h2[r, :], wn[...]) + bn[...]
            z_out[r, :] = simplex_forward(v, g3[...], s3[...], ones)[2].astype(BF16)


def rollout(x, w_latent, wta, g1, s1, w_hidden, g2, s2, wn, bn, g3, s3):
    rows, width = x.shape
    latent, hidden = w_latent.shape[0], w_hidden.shape[-1]
    return pl.pallas_call(
        rollout_kernel,
        grid=(1,),
        in_specs=dynamics_specs(rows, width, latent, hidden),
        out_shape=jax.ShapeDtypeStruct((rows, latent), BF16),
        out_specs=pl.BlockSpec((rows, latent), lambda k: (0, 0)),
        scratch_shapes=scratch(rows, hidden, True),
        compiler_params=pltpu.CompilerParams(vmem_limit_bytes=VMEM_BYTES),
    )(x, w_latent, wta, g1, s1, w_hidden, g2, s2, wn, bn, g3, s3)


def dynamics_kernel(
    x, wl, wta, g1, s1, w2, g2, s2, wn, bn, g3, s3, goal, weights, upstream,
    u, dx, z_out, loss, small, small3,
    p0, p1, p2, pre3, h1, h2, m1, m2, x1, x2, r1, r2, d1, d2, d3,
):
    pre = (p0, p1, p2)
    w2, g1, s1, g2, s2 = (ref.at[0] for ref in (w2, g1, s1, g2, s2))
    sums = [small.at[pl.ds(8 * i, 8)] for i in range(4)]
    small[...] = jnp.zeros_like(small)
    ones = group_matrix()
    width = wn.shape[1]
    forward_pair(x, wl, wta, g1, s1, w2, g2, s2, pre, h1, m1, x1, r1, h2, m2, x2, r2)
    totals = [None, None, None]
    count = x.shape[0] // TILE
    for i in range(count):
        r = tile_rows(i)
        pre3[r, :] = nn(h2[r, :], wn[...]) + bn[...]
    for start in range(0, x.shape[0], 64):
        r = slice(start, start + 64)
        y, inverse, z = simplex_forward(pre3[r, :], g3[...], s3[...], ones)
        z_out[r, :] = z.astype(BF16)
        differ = z - goal[r, :].astype(F32)
        weight = weights[r, :]
        loss[r, :] = weight * (
            CONSISTENCY / width * jnp.sum(differ * differ, axis=-1, keepdims=True)
        )
        grad = upstream[r, :].astype(F32) + weight * (2.0 * CONSISTENCY / width) * differ
        grad = grad * z
        dv = grad - z * group_sum(grad, ones)
        dvy = dv * y
        dy = dv * g3[...]
        mean = jnp.sum(dy, axis=-1, keepdims=True) * (1.0 / width)
        along = jnp.sum(dy * y, axis=-1, keepdims=True) * (1.0 / width)
        result = ((dy - mean - y * along) * inverse).astype(BF16)
        d3[r, :] = result
        for q, part in enumerate((dvy, dv, result.astype(F32))):
            part = functools.reduce(jnp.add, [part[s : s + 8] for s in range(0, 64, 8)])
            totals[q] = part if totals[q] is None else totals[q] + part
    for q in range(3):
        small3[8 * q : 8 * q + 8, :] = totals[q]

    def back_in(i):
        pre[i][...] = nt(d3[tile_rows(i), :], wn[...])

    backward_pair(
        x, wl, wta, g1, w2, g2, pre, m1, x1, r1, m2, x2, r2, d1, d2, back_in, dx, False, *sums
    )
    weight_grads(x, h1, d1, d2, h2, d3, u)


def dynamics(
    x, w_latent, wta, g1, s1, w_hidden, g2, s2, wn, bn, g3, s3, goal, weights, upstream
):
    rows, width = x.shape
    latent, hidden = w_latent.shape[0], w_hidden.shape[-1]
    held = scratch(rows, hidden)

    def whole(shape):
        return pl.BlockSpec(shape, lambda k: (0, 0))

    shapes = [
        ((hidden, hidden + width + latent), BF16),
        ((rows, width), F32),
        ((rows, latent), BF16),
        ((rows, 1), F32),
        ((32, hidden), F32),
        ((24, latent), F32),
    ]
    return pl.pallas_call(
        dynamics_kernel,
        grid=(1,),
        in_specs=dynamics_specs(rows, width, latent, hidden)
        + [whole((rows, latent)), whole((rows, 1)), whole((rows, latent))],
        out_shape=[jax.ShapeDtypeStruct(*s) for s in shapes],
        out_specs=[whole(s[0]) for s in shapes],
        scratch_shapes=held[:3]
        + [pltpu.VMEM((rows, latent), F32)]
        + held[3:]
        + [pltpu.VMEM((rows, latent), BF16)],
        compiler_params=pltpu.CompilerParams(vmem_limit_bytes=VMEM_BYTES),
    )(x, w_latent, wta, g1, s1, w_hidden, g2, s2, wn, bn, g3, s3, goal, weights, upstream)


def on_device(
    latents, actions, tasks, masks, reward_bins, reward_frac, value_bins, value_frac, targets,
    task_table, w_latent, w_action, w_task, gain_one, shift_one, w_hidden, gain_two, shift_two,
    w_next, bias_next, gain_three, shift_three, w_head, bias_head,
):
    section = lax.axis_index("section")
    device = lax.axis_index("batch")
    devices = lax.axis_size("batch")
    sections = lax.axis_size("section")
    rows, latent = latents.shape
    branches, hidden = w_hidden.shape[1], w_hidden.shape[-1]
    heads_count, bins = w_head.shape[1], w_head.shape[-1]
    tasks_count, task_dim = task_table.shape
    act = actions.shape[-1]
    scale = 1.0 / (rows * devices)
    rho = jnp.where(section == 0, 1.0, RHO).astype(F32)
    spare = LANES - task_dim - act

    ids = lax.broadcasted_iota(jnp.int32, (1, tasks_count), 1)
    one_hot = (tasks[:, None] == ids).astype(BF16)
    embedded = nn(one_hot, task_table).astype(BF16)
    extra = jnp.concatenate([embedded, actions[0], jnp.zeros((rows, spare), BF16)], axis=1)
    wta = jnp.concatenate(
        [w_task[0], w_action[0], jnp.zeros((spare, branches * hidden), BF16)], axis=0
    )
    weight = rho * masks[0].astype(F32)
    wide = LANES - bins
    wh = jnp.pad(w_head[0], ((0, 0), (0, 0), (0, wide)))
    bh = jnp.pad(bias_head[0], ((0, 0), (0, wide)), constant_values=-1e30)[:, None, :]
    none = jnp.zeros((2, rows), F32)
    cond = jnp.stack(
        [
            jnp.stack([reward_bins[0], value_bins[0]]).astype(F32),
            jnp.stack([reward_frac[0], value_frac[0]]),
            jnp.stack([weight, weight / (heads_count - 1)]),
        ]
        + [none] * 5,
        axis=-1,
    )
    g1 = gain_one[0].reshape(branches, 1, hidden)
    s1 = shift_one[0].reshape(branches, 1, hidden)
    g2 = gain_two[0][:, None, :]
    s2 = shift_two[0][:, None, :]
    shared = (w_latent[0], wta, g1, s1, w_hidden[0], g2, s2)
    last = (w_next[0], bias_next, gain_three, shift_three)

    first = rollout(jnp.concatenate([latents, extra], axis=1), *shared, *last)
    received = lax.ppermute(first, "section", [(i, i + 1) for i in range(sections - 1)])
    x = jnp.concatenate([jnp.where(section == 0, latents, received), extra], axis=1)
    u_heads, dx_heads, head_bias, loss, small = heads(x, *shared, wh, bh, cond)

    def run(upstream):
        return tuple(
            dynamics(x, *shared, *last, targets[0], weight[:, None], upstream)
        )

    empty = jnp.zeros((rows, latent), BF16)
    shapes = jax.eval_shape(run, empty)
    done = lax.cond(
        section == sections - 1,
        lambda: run(empty),
        lambda: tuple(jnp.zeros(s.shape, s.dtype) for s in shapes),
    )
    back = (dx_heads[:, :latent] + done[1][:, :latent]).astype(BF16)
    upstream = lax.ppermute(back, "section", [(i + 1, i) for i in range(sections - 1)])
    u_next, dx_next, z_out, loss_next, small_next, small3 = lax.cond(
        section == sections - 1, lambda: done, lambda: run(upstream)
    )

    dx = dx_heads + dx_next
    grads = dx[:, :latent].astype(BF16)
    table = jnp.einsum(
        "rt,re->te", one_hot.astype(F32), dx[:, latent : latent + task_dim], precision=HIGH
    )
    loss_sum = jnp.sum(loss) + jnp.sum(loss_next)

    width = x.shape[1]
    sum_heads = lax.psum_scatter(u_heads, "batch", scatter_dimension=1, tiled=True).astype(F32)
    sum_next = lax.psum_scatter(u_next, "batch", scatter_dimension=0, tiled=True).astype(F32)
    part = hidden // devices
    layer_one = jnp.concatenate(
        [sum_next[None, :, hidden : hidden + width], sum_heads[:, :, hidden : hidden + width]]
    )
    blocks = []
    inverse = pow(branches, -1, devices)
    for slot in range(branches):
        owner = lax.rem((device - slot + devices * branches) * inverse, devices)
        chosen = (branches * owner + slot) // devices
        piece = lax.dynamic_index_in_dim(layer_one, chosen, 0, keepdims=False)
        route = [((branches * e + slot) % devices, e) for e in range(devices)]
        blocks.append(lax.ppermute(piece.astype(BF16), "batch", route).astype(F32))
    w_one = jnp.concatenate(blocks, axis=0).T * scale

    small = jnp.concatenate([small_next[None], small]).reshape(branches, 4, 8, hidden).sum(2)
    small3 = small3.reshape(3, 8, latent).sum(1)
    packed = jnp.concatenate(
        [
            small[:, 0].reshape(devices, -1),
            small[:, 1].reshape(devices, -1),
            small[:, 2].reshape(branches, devices, part).swapaxes(0, 1).reshape(devices, -1),
            small[:, 3].reshape(branches, devices, part).swapaxes(0, 1).reshape(devices, -1),
            small3.reshape(3, devices, -1).swapaxes(0, 1).reshape(devices, -1),
        ],
        axis=1,
    )
    packed = lax.psum_scatter(packed, "batch", scatter_dimension=0, tiled=True)[0] * scale
    one = branches * hidden // devices
    two = branches * part
    three = latent // devices
    parts = jnp.split(packed, [one, 2 * one, 2 * one + two, 2 * one + 2 * two])
    third = parts[4].reshape(3, three)

    head_bias_total, loss_total = lax.psum((head_bias[:, 0, :bins], loss_sum), "batch")
    table_total = lax.psum(table, ("section", "batch"))
    w_two = jnp.concatenate([sum_next[None, :, :hidden], sum_heads[:, :, :hidden]])
    return (
        z_out[None],
        grads[None],
        (loss_total * scale).reshape(1),
        w_one[None, :latent],
        w_one[None, latent + task_dim : latent + task_dim + act],
        w_one[None, latent : latent + task_dim],
        parts[0][None],
        parts[1][None],
        (w_two.swapaxes(1, 2) * scale)[None],
        parts[2].reshape(1, branches, part),
        parts[3].reshape(1, branches, part),
        (sum_next[:, hidden + width :] * scale)[None],
        third[2][None],
        third[0][None],
        third[1][None],
        (sum_heads[:, :, hidden + width : hidden + width + bins] * scale)[None],
        (head_bias_total * scale)[None],
        table_total * scale,
    )


def solution(mesh):
    rows = P("section", "batch")
    wide = P("section", "batch", None)
    matrix = P("section", None, None)
    vector = P("section", None)
    in_specs = (
        P("batch", None), wide, P("batch"), rows, rows, rows, rows, rows, wide, P(),
        matrix, matrix, matrix, vector, vector, P("section", None, None, None), matrix, matrix,
        matrix, vector, vector, vector, P("section", None, None, None), matrix,
    )
    columns = P("section", None, "batch")
    out_specs = (
        wide, wide, P("section"), columns, columns, columns, rows, rows,
        P("section", None, None, "batch"), columns, columns, wide, rows, rows, rows,
        P("section", None, "batch", None), matrix, P(),
    )
    return jax.shard_map(
        on_device, mesh=mesh, in_specs=in_specs, out_specs=out_specs, check_vma=False
    )
```

time: 1640 us -> 672 us (0.41)
  matrix products: 527 us -> 2.6 us
  other arithmetic: 304 us -> 19.3 us
  local copies, waits for them, and re-layouts: 188 us -> 34.5 us
  Pallas kernels: 0 us -> 141 us
  waiting for transfers between devices: 470 us -> 340 us
  blocking collectives: 97.1 us -> 70.3 us
    dot_general x91 -> x2, matrix products: 527 us -> 2.6 us  [the longest x1 1.6 us: on_device(): jnp.einsum('rt,re->te', one_hot.astype(F32), dx[:, latent:latent + task_d...]
    reduce_sum x71 -> x4, other arithmetic: 181 us -> 3.82 us  [the longest x2 2.4 us: on_device(): loss_sum = jnp.sum(loss) + jnp.sum(loss_next)]
    pallas_call x0 -> x3, Pallas kernels: none -> 141 us  [the longest x1 103 us: heads(): pl.pallas_call(heads_kernel, grid=(count,), in_specs=[pl.BlockSpec((rows,...]
    reduce_scatter x4 -> x2, waiting for transfers between devices: 431 us -> 297 us  [the longest x1 221 us: on_device(): lax.psum_scatter(u_heads, 'batch', scatter_dimension=1, tiled=True)]
    convert_element_type x8 -> x6, other arithmetic: 52.2 us -> 3.8 us  [the longest x1 2.27 us: on_device(): back = (dx_heads[:, :latent] + done[1][:, :latent]).astype(BF16)]
    add x14 -> x0, local copies, waits for them, and re-layouts: 43.3 us -> none  [the longest x4 33.7 us: on_device(): matmul('rl,lh->rh', latent_in, latent_w)]
    reshape x4 -> x6, local copies, waits for them, and re-layouts: 33.4 us -> 1.63 us  [the longest x1 0.66 us: on_device(): parts[3].reshape(1, branches, part)]
    psum x2, blocking collectives: 97.1 us -> 70.3 us  [the longest x1 37.3 us: on_device(): table_total = lax.psum(table, ('section', 'batch'))]
  transfers between devices with their start and end apart: 14 -> 12, of which waited for: 8 -> 6; matrix products, arithmetic and copies ran while one was open for 20% -> 5% of each run, Pallas kernels for 0% -> 0%
where the time goes in v1:
time: 672 us; the launch traced here: 662 us
  waiting for transfers between devices  340 us (51%)
  Pallas kernels  141 us (21%)
  blocking collectives  70.3 us (10%)
  local copies, waits for them, and re-layouts  34.5 us (5%)
  starting transfers between devices  24.4 us (4%)
  other arithmetic  19.3 us (3%)
  between operations  17.9 us (3%)
  loops' own time  11.5 us (2%)
    reduce_scatter x1, waiting for transfers between devices, on_device(): lax.psum_scatter(u_heads, 'batch', scatter_dimension=1, tiled=True)  221 us
    pallas_call x1, Pallas kernels, heads(): pl.pallas_call(heads_kernel, grid=(count,), in_specs=[pl.BlockSpec((rows,...  103 us
    reduce_scatter x1, waiting for transfers between devices, on_device(): lax.psum_scatter(u_next, 'batch', scatter_dimension=0, tiled=True)  76 us
    psum x1, blocking collectives, on_device(): table_total = lax.psum(table, ('section', 'batch'))  37.3 us
    ppermute x1, waiting for transfers between devices, on_device(): lax.ppermute(back, 'section', [(i + 1, i) for i in range(sections - 1)])  34.2 us
    psum x1, blocking collectives, on_device(): lax.psum((head_bias[:, 0, :bins], loss_sum), 'batch')  33.1 us
    pallas_call x1, Pallas kernels, dynamics(): pl.pallas_call(dynamics_kernel, grid=(1,), in_specs=dynamics_specs(rows,...  24.6 us
    ppermute x7, starting transfers between devices, on_device(): blocks.append(lax.ppermute(piece.astype(BF16), 'batch', route).astype(F32))  17.3 us
  transfers between devices with their start and end apart: 12, of which 6 were waited for; matrix products, arithmetic and copies ran while one was open for 5% of the time, Pallas kernels for 0%

profile of v1, /device:TPU:0, one launch (start us, length us, event | category | flops | bytes accessed | tf_op | source)
XLA Modules:
  0.0 662.1 jit_solution(10381529986229996170)
XLA Ops:
  7.4 0.9 copy.108
  8.4 1.0 convolution_convert_fusion
  9.5 1.9 maximum_maximum_fusion.wta
  11.4 1.2 fusion.1.x
  12.8 13.5 %shard_map.367 = bf16[768,512]{1,0:T(8,128)(2,1)} custom-call(bf16[768,640]{1,0:T(8,128)(2,1)} %fusion.1.x, bf16[512,7168]{1,0:T(8,128)(2,1)} %bitcast.84, bf16[128,7168]{1,0:T(8,128)(2,1)S(1)} %maximum_maximum_fusion.wta, f32[7,1,1024]{2,1,0:T(1,128)S(1)} %bitcast.100, f32[7,1,1024]{2,1,0:T(1,128)S(1)} %bitcast.104, bf16[7,1024,1024]{2,1,0:T(8,128)(2,1)} %bitcast.80, ...), custom_call_target="tpu_custom_call" | custom-call | tf_op jit(solution)/shard_map/pallas_call | solution.py:315
  26.2 5.7 collective-permute-start
  32.6 1.2 copy.113
  33.8 1.2 copy.112
  35.0 1.2 copy.114
  36.2 1.9 copy.109
  38.1 1.5 pad.8.wh
  39.6 0.9 stack.35
  40.5 1.0 stack_broadcast_in_dim.3
  41.5 4.0 stack.36.cond
  45.5 2.6 collective-permute-done
  48.6 17.4 %conditional.2 = (bf16[1024,2176]{1,0:T(8,128)(2,1)}, f32[768,640]{1,0:T(8,128)}, bf16[768,512]{1,0:T(8,128)(2,1)}, f32[32,1024]{1,0:T(8,128)S(1)}, f32[24,512]{...) conditional(s32[]{:T(128)} %convert_element_type.86, () %tuple.29, ...), branch_computations={%region_0.1_spmd, %region_1.2_spmd} | conditional | bytes 8965200 | solution.py:467
  48.6 0.9 broadcast.42
  49.6 1.3 broadcast.50
  50.9 1.4 broadcast.41
  52.3 2.4 broadcast.40
  66.0 103.2 %shard_map.368 = (bf16[6,1024,1792]{2,1,0:T(8,128)(2,1)}, f32[768,640]{1,0:T(8,128)}, f32[6,8,128]{2,1,0:T(8,128)}, f32[768,1]{1,0:T(8,128)}, f32[6,32,1024]{2,1,0:T(8,128)}) custom-call(bf16[768,640]{1,0:T(8,128)(2,1)S(1)} %fusion.2.x, bf16[512,7168]{1,0:T(8,128)(2,1)} %bitcast.86, bf16[128,7168]{1,0:T(8,128)(2,1)S(1)} %maximum_maximum_fusion.wta, ...), custom_call_target="tpu_custom_call" | custom-call | tf_op jit(solution)/shard_map/pallas_call | solution.py:240
  169.2 2.3 add_convert_fusion
  171.5 1.3 collective-permute-start.1
  172.8 34.2 %collective-permute-done.1 = bf16[768,512]{1,0:T(8,128)(2,1)S(1)} collective-permute-done((bf16[768,512]{1,0:T(8,128)(2,1)S(1)}, bf16[768,512]{1,0:T(8,128)(2,1)S(1)}, u32[]{:S(2)}, u32[]{:S(2)}) %collective-permute-start.1) | collective-permute-done | bytes 786464 | tf_op jit(solution)/shard_map/ppermute | solution.py:473
  207.0 27.4 %conditional.3 = (bf16[1024,2176]{1,0:T(8,128)(2,1)}, f32[768,640]{1,0:T(8,128)}, f32[24,512]{1,0:T(8,128)S(1)}, bf16[1,768,512]{2,1,0:T(8,128)(2,1)}, f32[]{:T(128)}, /*index=5*/f32[1,4,8,1024]{3,2,1,0:T(8,128)S(1)}) conditional(s32[]{:T(128)} %convert_element_type.86, (bf16[1,768,512]{2,1,0:T(8,128)(2,1)S(1)}, f32[768]{0:T(1024)S(1)}, ...), branch_computations={%region_2.3_spmd, %region_3.4_spmd} | conditional | flops 767 | bytes 8916024 | solution.py:474
  207.0 0.9 broadcast_in_dim.72.weights
  207.9 24.6 %branch_0_fun.1 = (bf16[1024,2176]{1,0:T(8,128)(2,1)}, f32[768,640]{1,0:T(8,128)}, bf16[768,512]{1,0:T(8,128)(2,1)}, f32[768,1]{1,0:T(8,128)}, f32[32,1024]{1,0:T(8,128)S(1)}, /*index=5*/f32[24,512]{1,0:T(8,128)S(1)}) custom-call(bf16[768,640]{1,0:T(8,128)(2,1)S(1)} %get-tuple-element.106.x, bf16[512,7168]{1,0:T(8,128)(2,1)} %get-tuple-element.107.wl, ...), custom_call_target="tpu_custom_call" | custom-call | tf_op jit(solution)/shard_map/cond/branch_0_fun/pallas_call | solution.py:394
  232.5 1.7 reduce_sum.43
  234.6 1.4 maximum_reduce_fusion
  236.8 0.7 concatenate.51
  237.6 0.7 reduce-scatter.3.cloned.1.call-update
  238.4 0.6 reduce-scatter.5.cloned.1.call-update
  239.9 0.7 reduce_sum.39
  240.6 0.7 slice.96
  242.6 33.1 %all-reduce.3 = (f32[]{:T(128)}, f32[6,101]{1,0:T(8,128)S(1)}) all-reduce(f32[]{:T(128)S(6)} %add.113, f32[6,101]{1,0:T(8,128)S(1)} %bitcast.120), channel_id=1, replica_groups=mesh['section'=2,'batch'=16] {'batch'}, use_global_device_ids=true, to_apply=%region_6.7 | all-reduce | flops 607 | bytes 4856 | tf_op jit(solution)/shard_map/psum | solution.py:521
  275.7 3.1 add.112
  280.0 1.6 fusion.4
  281.6 37.3 %psum.23 = f32[80,96]{1,0:T(8,128)S(1)} all-reduce(f32[80,96]{1,0:T(8,128)S(1)} %fusion.4), channel_id=1, replica_groups=mesh['section'=2,'batch'=16] {'section','batch'}, use_global_device_ids=true, to_apply=%region_13.14 | all-reduce | flops 7680 | bytes 61440 | tf_op jit(solution)/shard_map/psum | solution.py:522
  318.9 0.6 broadcast_multiply_fusion
  319.5 2.4 fusion.3
  321.9 2.6 all-reduce.6.cloned.1.call-done
  324.5 1.5 dynamic-slice_multiply_fusion
  326.0 0.7 slice_reduce_fusion.4
  326.7 0.7 reshape.136
  327.3 0.7 reshape.135
  328.0 0.6 fusion.31
  328.6 76.0 %reduce-scatter.3.cloned.1.call-done = bf16[64,2176]{1,0:T(8,128)(2,1)} async-done(((bf16[1024,2176]{1,0:T(8,128)(2,1)}), bf16[64,2176]{1,0:T(8,128)(2,1)}) %reduce-scatter.3.cloned.1.call-update) | async-done | bytes 278544 | tf_op jit(solution)/shard_map/reduce_scatter | solution.py:487
  404.6 1.0 convert_element_type.91
  405.6 0.7 fusion.23
  406.3 220.7 %reduce-scatter.5.cloned.1.call-done = bf16[6,64,1792]{2,1,0:T(8,128)(2,1)} async-done(((bf16[6,1024,1792]{2,1,0:T(8,128)(2,1)}), bf16[6,64,1792]{2,1,0:T(8,128)(2,1)}) %reduce-scatter.5.cloned.1.call-update) | async-done | bytes 1376272 | tf_op jit(solution)/shard_map/reduce_scatter | solution.py:486
  627.0 1.2 slice.102
  628.4 2.7 collective-permute-start.8
  631.2 0.7 collective-permute-start.2
  631.8 1.5 collective-permute-start.3
  633.4 5.3 collective-permute-start.4
  638.7 3.3 collective-permute-start.5
  642.2 0.7 fusion.6
  643.1 1.5 fusion
  644.6 1.9 collective-permute-start.6
  646.6 1.9 collective-permute-start.7
  648.5 2.9 collective-permute-done.6
  651.7 1.0 slice_bitcast_fusion
  652.7 0.8 copy.120
  653.5 0.7 copy.119
  (123 shorter events, 4.8 us)
Async XLA Ops:
  7.2 1.2 copy-start
  7.2 4.2 copy-start.9
  7.2 317.3 %all-reduce.6.cloned.1.call-start = ((), (), s32[]{:S(2)}) async-start(), calls=%async_computation.4 | async-start | bytes 245760
  8.4 4.2 copy-start.12
  9.4 3.2 copy-start.14
  9.4 3.2 copy-start.2
  9.4 3.2 copy-start.16
  9.4 3.2 copy-start.17
  9.4 3.2 copy-start.18
  9.4 3.2 copy-start.19
  9.5 3.2 copy-start.21
  9.5 3.2 copy-start.22
  9.5 3.2 copy-start.23
  12.7 19.3 %copy-start.25 = (f32[1,6,101]{2,0,1:T(1,128)S(1)}, f32[1,6,101]{2,0,1:T(1,128)}, u32[]{:S(2)}) copy-start(f32[1,6,101]{2,0,1:T(1,128)} %param.51) | copy-start | bytes 7276
  12.7 19.9 %copy-start.27 = (f32[1,768]{1,0:T(1,128)S(1)}, f32[1,768]{1,0:T(1,128)}, u32[]{:S(2)}) copy-start(f32[1,768]{1,0:T(1,128)} %param.35) | copy-start | bytes 9220
  12.7 19.8 %copy-start.28 = (f32[1,768]{1,0:T(1,128)S(1)}, f32[1,768]{1,0:T(1,128)}, u32[]{:S(2)}) copy-start(f32[1,768]{1,0:T(1,128)} %param.33) | copy-start | bytes 9220
  12.7 21.0 %copy-start.29 = (s32[1,768]{1,0:T(1,128)S(1)}, s32[1,768]{1,0:T(1,128)}, u32[]{:S(2)}) copy-start(s32[1,768]{1,0:T(1,128)} %param.34) | copy-start | bytes 9220
  12.7 21.0 %copy-start.30 = (s32[1,768]{1,0:T(1,128)S(1)}, s32[1,768]{1,0:T(1,128)}, u32[]{:S(2)}) copy-start(s32[1,768]{1,0:T(1,128)} %param.32) | copy-start | bytes 9220
  12.7 22.2 %copy-start.26 = (s32[1,768]{1,0:T(1,128)S(1)}, s32[1,768]{1,0:T(1,128)}, u32[]{:S(2)}) copy-start(s32[1,768]{1,0:T(1,128)} %param.31) | copy-start | bytes 9220
  26.2 21.9 %collective-permute-start = (bf16[768,512]{1,0:T(8,128)(2,1)}, bf16[768,512]{1,0:T(8,128)(2,1)}, u32[]{:S(2)}, u32[]{:S(2)}) collective-permute-start(bf16[768,512]{1,0:T(8,128)(2,1)} %shard_map.367), channel_id=1, source_target_pairs={{0,16},{1,17},{2,18},{3,19},{4,20},{5,21},{6,22},{7,23},{8,24},{9,... | collective-permute-start | bytes 2359304 | tf_op jit(solution)/shard_map/ppermute | solution.py:456
  39.6 1.9 copy-start.11
  41.5 6.7 %copy-start.10 = (bf16[768,512]{1,0:T(8,128)(2,1)S(1)}, bf16[768,512]{1,0:T(8,128)(2,1)}, u32[]{:S(2)}) copy-start(bf16[768,512]{1,0:T(8,128)(2,1)} %param.28) | copy-start | bytes 2359300
  45.5 2.7 copy-start.13
  45.5 2.7 copy-start.15
  45.5 3.0 copy-start.3
  45.5 3.0 copy-start.7
  169.2 37.8 %copy-start.4 = (bf16[1,1024,512]{2,1,0:T(8,128)(2,1)S(1)}, bf16[1,1024,512]{2,1,0:T(8,128)(2,1)}, u32[]{:S(2)}) copy-start(bf16[1,1024,512]{2,1,0:T(8,128)(2,1)} %param.46) | copy-start | bytes 3145732
  169.2 37.8 %copy-start.8 = (bf16[1,768,512]{2,1,0:T(8,128)(2,1)S(1)}, bf16[1,768,512]{2,1,0:T(8,128)(2,1)}, u32[]{:S(2)}) copy-start(bf16[1,768,512]{2,1,0:T(8,128)(2,1)} %param.36) | copy-start | bytes 2359300
  171.5 35.5 %collective-permute-start.1 = (bf16[768,512]{1,0:T(8,128)(2,1)S(1)}, bf16[768,512]{1,0:T(8,128)(2,1)S(1)}, u32[]{:S(2)}, u32[]{:S(2)}) collective-permute-start(bf16[768,512]{1,0:T(8,128)(2,1)S(1)} %add_convert_fusion), channel_id=1, source_target_pairs={{16,0},{17,1},{18,2},{19,3},{20,4},{21,5},{22,6},{23,7},{24,8},{25... | collective-permute-start | bytes 2359304 | tf_op jit(solution)/shard_map/ppermute | solution.py:473
  237.6 167.0 %reduce-scatter.3.cloned.1.call-start = ((), (), s32[]{:S(2)}) async-start(), calls=%async_computation.2 | async-start | bytes 4734976 | tf_op jit(solution)/shard_map/reduce_scatter | solution.py:487
  238.3 388.6 %reduce-scatter.5.cloned.1.call-start = ((), (), s32[]{:S(2)}) async-start(), calls=%async_computation.3 | async-start | bytes 23396352 | tf_op jit(solution)/shard_map/reduce_scatter | solution.py:486
  238.4 0.9 copy-start.31
  238.4 1.5 copy-start.20
  238.4 37.3 %copy-start.6 = (f32[768,640]{1,0:T(8,128)S(1)}, f32[768,640]{1,0:T(8,128)}, u32[]{:S(2)}) copy-start(f32[768,640]{1,0:T(8,128)} %get-tuple-element.151) | copy-start | bytes 5898244
  275.7 4.3 copy-start.24
  627.0 15.0 %copy-start.5 = (bf16[6,64,1792]{2,1,0:T(8,128)(2,1)S(1)}, bf16[6,64,1792]{2,1,0:T(8,128)(2,1)}, u32[]{:S(2)}) copy-start(bf16[6,64,1792]{2,1,0:T(8,128)(2,1)} %reduce-scatter.5.cloned.1.call-done) | copy-start | bytes 4128772
  628.4 23.0 %collective-permute-start.8 = (bf16[64,640]{1,0:T(8,128)(2,1)S(1)}, bf16[64,640]{1,0:T(8,128)(2,1)S(1)}, u32[]{:S(2)}, u32[]{:S(2)}) collective-permute-start(bf16[64,640]{1,0:T(8,128)(2,1)S(1)} %get-tuple-element.316), channel_id=1, source_target_pairs={{6,0},{13,1},{4,2},{11,3},{2,4},{9,5},{0,6},{7,7},{14,8},{5,9},{12... | collective-permute-start | bytes 245768 | tf_op jit(solution)/shard_map/ppermute | solution.py:499
  631.2 13.4 %collective-permute-start.2 = (bf16[64,640]{1,0:T(8,128)(2,1)S(1)}, bf16[64,640]{1,0:T(8,128)(2,1)S(1)}, u32[]{:S(2)}, u32[]{:S(2)}) collective-permute-start(bf16[64,640]{1,0:T(8,128)(2,1)S(1)} %get-tuple-element.317), channel_id=1, source_target_pairs={{0,0},{7,1},{14,2},{5,3},{12,4},{3,5},{10,6},{1,7},{8,8},{15,9},{6... | collective-permute-start | bytes 245768 | tf_op jit(solution)/shard_map/ppermute | solution.py:499
  631.8 14.7 %collective-permute-start.3 = (bf16[64,640]{1,0:T(8,128)(2,1)S(1)}, bf16[64,640]{1,0:T(8,128)(2,1)S(1)}, u32[]{:S(2)}, u32[]{:S(2)}) collective-permute-start(bf16[64,640]{1,0:T(8,128)(2,1)S(1)} %get-tuple-element.318), channel_id=1, source_target_pairs={{1,0},{8,1},{15,2},{6,3},{13,4},{4,5},{11,6},{2,7},{9,8},{0,9},{7,... | collective-permute-start | bytes 245768 | tf_op jit(solution)/shard_map/ppermute | solution.py:499
  633.4 15.1 %collective-permute-start.4 = (bf16[64,640]{1,0:T(8,128)(2,1)S(1)}, bf16[64,640]{1,0:T(8,128)(2,1)S(1)}, u32[]{:S(2)}, u32[]{:S(2)}) collective-permute-start(bf16[64,640]{1,0:T(8,128)(2,1)S(1)} %get-tuple-element.319), channel_id=1, source_target_pairs={{2,0},{9,1},{0,2},{7,3},{14,4},{5,5},{12,6},{3,7},{10,8},{1,9},{8,... | collective-permute-start | bytes 245768 | tf_op jit(solution)/shard_map/ppermute | solution.py:499
  638.7 9.8 %collective-permute-start.5 = (bf16[64,640]{1,0:T(8,128)(2,1)S(1)}, bf16[64,640]{1,0:T(8,128)(2,1)S(1)}, u32[]{:S(2)}, u32[]{:S(2)}) collective-permute-start(bf16[64,640]{1,0:T(8,128)(2,1)S(1)} %get-tuple-element.320), channel_id=1, source_target_pairs={{3,0},{10,1},{1,2},{8,3},{15,4},{6,5},{13,6},{4,7},{11,8},{2,9},{9... | collective-permute-start | bytes 245768 | tf_op jit(solution)/shard_map/ppermute | solution.py:499
  644.6 6.8 %collective-permute-start.6 = (bf16[64,640]{1,0:T(8,128)(2,1)S(1)}, bf16[64,640]{1,0:T(8,128)(2,1)S(1)}, u32[]{:S(2)}, u32[]{:S(2)}) collective-permute-start(bf16[64,640]{1,0:T(8,128)(2,1)S(1)} %get-tuple-element.321), channel_id=1, source_target_pairs={{4,0},{11,1},{2,2},{9,3},{0,4},{7,5},{14,6},{5,7},{12,8},{3,9},{10... | collective-permute-start | bytes 245768 | tf_op jit(solution)/shard_map/ppermute | solution.py:499
  646.6 4.8 collective-permute-start.7
  651.4 2.8 copy-start.1
Sparse Core Ops, SparseCore 0:
  237.7 86.7 all-reduce.5
  328.4 76.1 reduce-scatter.2
  409.4 217.5 reduce-scatter.4
